TPU v7x, 256 devices: a whole 4x4x8 slice. The times are simulated.
256 devices in a mesh: prow: 8 (over x, core), pcol: 32 (over z, y).
Axes of the slice: x: 4, y: 4, z: 8, core: 2. Of those that a mesh axis runs over, the one named last changes fastest.
Arguments:
- matrix: bfloat16 [4, 8, 512, 1, 32, 512], P(None, 'prow', None, None, 'pcol'), may hold values from -6 to 6
- upper_inv: bfloat16 [2, 512, 512], replicated, may hold values from -4 to 4
- lower_inv: bfloat16 [2, 512, 512], replicated, may hold values from -4 to 4
- solution: bfloat16 [1, 32, 512], P(None, 'pcol'), may hold values from -0.046875 to 0.046875
- right_side: float32 [4, 8, 512], P(None, 'prow'), may hold values from -6 to 6
- diagonal_block_inverses: bfloat16 [1, 8, 512, 512], P(None, 'prow'), may hold values from -0.009765625 to 0.009765625
Outputs:
- updated: bfloat16 [4, 8, 512, 1, 32, 512], P(None, 'prow', None, None, 'pcol')
- residual: float32 [4, 8, 512], P(None, 'prow')
- precond: float32 [8, 512], replicated
All inputs are finite; a program needn't handle non-finite values.
Results may differ from a plain program's by a relative error of at most 0.0085.
Values may be sent and summed in bfloat16 or wider, within the bound.
A program may use at most 128 MiB of HBM per device.

v0:
```python
import jax
import jax.numpy as jnp
from jax import lax
from jax.sharding import PartitionSpec as P

PANELS = 2


def broadcast(value, axis, source):
    kept = jnp.where(lax.axis_index(axis) == source, value, 0).astype(value.dtype)
    return lax.psum(kept, axis)


def shards(matrix, upper_inv, lower_inv, solution, right_side, diagonal_block_inverses):
    rows_blk = matrix.shape[0]
    cols_blk = matrix.shape[3]
    blk_width = matrix.shape[2]
    row_processors = lax.axis_size("prow")
    col_devs = lax.axis_size("pcol")
    col_index = lax.axis_index("pcol")
    base_matrix = matrix.reshape(rows_blk * blk_width, cols_blk * blk_width)
    current = base_matrix
    for section in range(PANELS):
        col_local = section // col_devs
        local_row_block = section // row_processors
        upper_tri = jnp.triu(upper_inv[section])
        lower_tri = jnp.tril(lower_inv[section])
        column = current
        row_band = current[local_row_block * blk_width : (local_row_block + 1) * blk_width, :]
        factored = jnp.dot(column, upper_tri, preferred_element_type=jnp.float32).astype(
            jnp.bfloat16
        )
        left_panel = broadcast(factored, "pcol", section % col_devs)
        top_local = jnp.dot(lower_tri, row_band, preferred_element_type=jnp.float32).astype(
            jnp.bfloat16
        )
        top_panel = broadcast(top_local, "prow", section % row_processors)
        current = (
            current.astype(jnp.float32)
            - jnp.dot(left_panel, top_panel, preferred_element_type=jnp.float32)
        ).astype(jnp.bfloat16)
    partial_value = jnp.dot(
        base_matrix, solution.reshape(cols_blk * blk_width), preferred_element_type=jnp.float32
    )
    totals = lax.psum(partial_value, "pcol")
    residual = right_side.reshape(rows_blk * blk_width) - totals
    res_blocks = residual.reshape(rows_blk, blk_width)
    slot_count = diagonal_block_inverses.shape[0]
    inverses = diagonal_block_inverses.reshape(slot_count, blk_width, blk_width)
    solve_count = slot_count * row_processors
    col_blocks = base_matrix.reshape(rows_blk * blk_width, cols_blk, blk_width)

    def carry_forward(blk_id, state):
        accum, solved = state
        owner_row = blk_id % row_processors
        slot_id = blk_id // row_processors
        pending = lax.dynamic_slice_in_dim(accum, slot_id * blk_width, blk_width, 0)
        res_block = lax.dynamic_slice_in_dim(res_blocks, slot_id, 1, 0)[0]
        inv_block = inverses[0].astype(jnp.float32)
        row_total = lax.psum(pending, "pcol")
        local_value = jnp.dot(inv_block, res_block - row_total, precision=lax.Precision.HIGHEST)
        new_value = broadcast(local_value, "prow", owner_row)
        rounded = new_value.astype(jnp.bfloat16)
        has_col = col_index == blk_id % col_devs
        col_piece = col_blocks[:, 0, :]
        product = jnp.dot(col_piece, rounded, preferred_element_type=jnp.float32)
        accum = accum + jnp.where(has_col, product, jnp.zeros_like(product))
        solved = lax.dynamic_update_slice_in_dim(solved, new_value[None], blk_id, 0)
        return (accum, solved)

    start = (
        jnp.zeros((rows_blk * blk_width,), jnp.float32),
        jnp.zeros((solve_count, blk_width), jnp.float32),
    )
    precond = lax.fori_loop(0, solve_count, carry_forward, start)[1]
    return (current.reshape(matrix.shape), residual.reshape(right_side.shape), precond)


def solution(mesh):
    return jax.shard_map(
        shards,
        mesh=mesh,
        in_specs=(
            P(None, "prow", None, None, "pcol", None),
            P(),
            P(),
            P(None, "pcol", None),
            P(None, "prow", None),
            P(None, "prow", None, None),
        ),
        out_specs=(P(None, "prow", None, None, "pcol", None), P(None, "prow", None), P()),
        check_vma=False,
    )
```

profile of v0, /device:TPU:1, one launch (start us, length us, event | category | flops | bytes accessed | tf_op | source)
XLA Modules:
  0.0 947.7 jit_solution(12790687416914332410)
XLA Ops:
  7.3 2.6 fusion.5
  10.0 2.9 fusion.3
  13.6 65.6 %psum.69 = f32[2048]{0:T(1024)S(1)} all-reduce(f32[2048]{0:T(1024)S(1)} %bitcast.79), channel_id=1, replica_groups=mesh['prow'=8,'pcol'=32] {'pcol'}, use_global_device_ids=true, to_apply=%region_4.5 | all-reduce | flops 2048 | bytes 16384 | tf_op jit(solution)/shard_map/psum | solution.py:45
  79.3 154.3 %all-reduce.5.cloned.1.call-done = bf16[2048,512]{0,1:T(8,128)(2,1)} async-done(((bf16[2048,512]{0,1:T(8,128)(2,1)}), bf16[2048,512]{0,1:T(8,128)(2,1)}) %all-reduce.5.cloned.1.call-update) | async-done | bytes 2097168 | tf_op jit(solution)/shard_map/psum | solution.py:11
  233.6 3.0 subtract_convert_fusion.1
  239.2 4.3 fusion.4
  244.6 691.6 %while.19 = (s32[]{:T(128)}, f32[2048]{0:T(1024)S(1)}, f32[8,512]{1,0:T(8,128)}, s32[]{:T(128)}, f32[4,512]{1,0:T(4,128)S(1)}, /*index=5*/bf16[1,1,512,512]{3,2,...) while((s32[]{:T(128)}, f32[2048]{0:T(1024)S(1)}, ...), condition=%wide.region_8.9_spmd.clone, body=%wide.region_5.8_spmd.clone.sunk | while | flops 5253665 | bytes 2712061 | solution.py:75
  244.7 58.2 %psum.74 = f32[512]{0:T(512)S(1)} all-reduce(f32[512]{0:T(512)S(1)} %dynamic_slice.28), channel_id=1, replica_groups=mesh['prow'=8,'pcol'=32] {'pcol'}, use_global_device_ids=true, to_apply=%region_6.6 | all-reduce | flops 512 | bytes 4096 | tf_op jit(solution)/shard_map/while/body/eval_jaxpr/psum | solution.py:60
  303.4 31.3 %psum.75 = f32[512]{0:T(512)S(1)} all-reduce(f32[512]{0:T(512)S(1)} %broadcast_select_fusion.5), channel_id=1, replica_groups=mesh['prow'=8,'pcol'=32] {'prow'}, use_global_device_ids=true, to_apply=%region_7.7 | all-reduce | flops 512 | bytes 4096 | tf_op jit(solution)/shard_map/while/body/eval_jaxpr/psum | solution.py:11
  336.7 55.7 %psum.74 = f32[512]{0:T(512)S(1)} all-reduce(f32[512]{0:T(512)S(1)} %dynamic_slice.28), channel_id=1, replica_groups=mesh['prow'=8,'pcol'=32] {'pcol'}, use_global_device_ids=true, to_apply=%region_6.6 | all-reduce | flops 512 | bytes 4096 | tf_op jit(solution)/shard_map/while/body/eval_jaxpr/psum | solution.py:60
  393.0 26.6 %psum.75 = f32[512]{0:T(512)S(1)} all-reduce(f32[512]{0:T(512)S(1)} %broadcast_select_fusion.5), channel_id=1, replica_groups=mesh['prow'=8,'pcol'=32] {'prow'}, use_global_device_ids=true, to_apply=%region_7.7 | all-reduce | flops 512 | bytes 4096 | tf_op jit(solution)/shard_map/while/body/eval_jaxpr/psum | solution.py:11
  421.7 57.8 %psum.74 = f32[512]{0:T(512)S(1)} all-reduce(f32[512]{0:T(512)S(1)} %dynamic_slice.28), channel_id=1, replica_groups=mesh['prow'=8,'pcol'=32] {'pcol'}, use_global_device_ids=true, to_apply=%region_6.6 | all-reduce | flops 512 | bytes 4096 | tf_op jit(solution)/shard_map/while/body/eval_jaxpr/psum | solution.py:60
  480.0 26.6 %psum.75 = f32[512]{0:T(512)S(1)} all-reduce(f32[512]{0:T(512)S(1)} %broadcast_select_fusion.5), channel_id=1, replica_groups=mesh['prow'=8,'pcol'=32] {'prow'}, use_global_device_ids=true, to_apply=%region_7.7 | all-reduce | flops 512 | bytes 4096 | tf_op jit(solution)/shard_map/while/body/eval_jaxpr/psum | solution.py:11
  508.7 55.7 %psum.74 = f32[512]{0:T(512)S(1)} all-reduce(f32[512]{0:T(512)S(1)} %dynamic_slice.28), channel_id=1, replica_groups=mesh['prow'=8,'pcol'=32] {'pcol'}, use_global_device_ids=true, to_apply=%region_6.6 | all-reduce | flops 512 | bytes 4096 | tf_op jit(solution)/shard_map/while/body/eval_jaxpr/psum | solution.py:60
  565.0 26.6 %psum.75 = f32[512]{0:T(512)S(1)} all-reduce(f32[512]{0:T(512)S(1)} %broadcast_select_fusion.5), channel_id=1, replica_groups=mesh['prow'=8,'pcol'=32] {'prow'}, use_global_device_ids=true, to_apply=%region_7.7 | all-reduce | flops 512 | bytes 4096 | tf_op jit(solution)/shard_map/while/body/eval_jaxpr/psum | solution.py:11
  593.6 57.2 %psum.74 = f32[512]{0:T(512)S(1)} all-reduce(f32[512]{0:T(512)S(1)} %dynamic_slice.28), channel_id=1, replica_groups=mesh['prow'=8,'pcol'=32] {'pcol'}, use_global_device_ids=true, to_apply=%region_6.6 | all-reduce | flops 512 | bytes 4096 | tf_op jit(solution)/shard_map/while/body/eval_jaxpr/psum | solution.py:60
  651.3 26.6 %psum.75 = f32[512]{0:T(512)S(1)} all-reduce(f32[512]{0:T(512)S(1)} %broadcast_select_fusion.5), channel_id=1, replica_groups=mesh['prow'=8,'pcol'=32] {'prow'}, use_global_device_ids=true, to_apply=%region_7.7 | all-reduce | flops 512 | bytes 4096 | tf_op jit(solution)/shard_map/while/body/eval_jaxpr/psum | solution.py:11
  680.0 55.7 %psum.74 = f32[512]{0:T(512)S(1)} all-reduce(f32[512]{0:T(512)S(1)} %dynamic_slice.28), channel_id=1, replica_groups=mesh['prow'=8,'pcol'=32] {'pcol'}, use_global_device_ids=true, to_apply=%region_6.6 | all-reduce | flops 512 | bytes 4096 | tf_op jit(solution)/shard_map/while/body/eval_jaxpr/psum | solution.py:60
  736.3 26.6 %psum.75 = f32[512]{0:T(512)S(1)} all-reduce(f32[512]{0:T(512)S(1)} %broadcast_select_fusion.5), channel_id=1, replica_groups=mesh['prow'=8,'pcol'=32] {'prow'}, use_global_device_ids=true, to_apply=%region_7.7 | all-reduce | flops 512 | bytes 4096 | tf_op jit(solution)/shard_map/while/body/eval_jaxpr/psum | solution.py:11
  764.9 57.2 %psum.74 = f32[512]{0:T(512)S(1)} all-reduce(f32[512]{0:T(512)S(1)} %dynamic_slice.28), channel_id=1, replica_groups=mesh['prow'=8,'pcol'=32] {'pcol'}, use_global_device_ids=true, to_apply=%region_6.6 | all-reduce | flops 512 | bytes 4096 | tf_op jit(solution)/shard_map/while/body/eval_jaxpr/psum | solution.py:60
  822.6 26.6 %psum.75 = f32[512]{0:T(512)S(1)} all-reduce(f32[512]{0:T(512)S(1)} %broadcast_select_fusion.5), channel_id=1, replica_groups=mesh['prow'=8,'pcol'=32] {'prow'}, use_global_device_ids=true, to_apply=%region_7.7 | all-reduce | flops 512 | bytes 4096 | tf_op jit(solution)/shard_map/while/body/eval_jaxpr/psum | solution.py:11
  851.3 55.7 %psum.74 = f32[512]{0:T(512)S(1)} all-reduce(f32[512]{0:T(512)S(1)} %dynamic_slice.28), channel_id=1, replica_groups=mesh['prow'=8,'pcol'=32] {'pcol'}, use_global_device_ids=true, to_apply=%region_6.6 | all-reduce | flops 512 | bytes 4096 | tf_op jit(solution)/shard_map/while/body/eval_jaxpr/psum | solution.py:60
  907.6 26.6 %psum.75 = f32[512]{0:T(512)S(1)} all-reduce(f32[512]{0:T(512)S(1)} %broadcast_select_fusion.5), channel_id=1, replica_groups=mesh['prow'=8,'pcol'=32] {'prow'}, use_global_device_ids=true, to_apply=%region_7.7 | all-reduce | flops 512 | bytes 4096 | tf_op jit(solution)/shard_map/while/body/eval_jaxpr/psum | solution.py:11
  936.2 5.0 subtract_convert_fusion
  (122 shorter events, 25.4 us)
Async XLA Ops:
  7.2 5.8 copy-start
  7.2 2.8 copy-start.1
  7.2 2.8 copy-start.6
  7.2 72.0 %all-reduce.7.cloned.1.call-start = ((), (), s32[]{:S(2)}) async-start(), calls=%async_computation.1 | async-start | bytes 1048576 | tf_op jit(solution)/shard_map/psum | solution.py:11
  9.9 223.7 %all-reduce.5.cloned.1.call-start = ((), (), s32[]{:S(2)}) async-start(), calls=%async_computation | async-start | bytes 4194304 | tf_op jit(solution)/shard_map/psum | solution.py:11
  12.8 66.3 %copy-start.4 = (f32[4,1,512]{2,1,0:T(1,128)S(1)}, f32[4,1,512]{2,1,0:T(1,128)}, u32[]{:S(2)}) copy-start(f32[4,1,512]{2,1,0:T(1,128)} %param.12) | copy-start | bytes 24580
  12.9 923.3 %all-reduce.11.cloned.1.call-start = ((), (), s32[]{:S(2)}) async-start(), calls=%async_computation.3 | async-start | bytes 1048576 | tf_op jit(solution)/shard_map/psum | solution.py:11
  79.2 157.4 %copy-start.3 = (f32[2048]{0:T(1024)}, f32[2048]{0:T(1024)S(1)}, u32[]{:S(2)}) copy-start(f32[2048]{0:T(1024)S(1)} %sub.28) | copy-start | bytes 24580
  79.2 158.7 %copy-start.5 = (bf16[2,512,512]{2,1,0:T(8,128)(2,1)S(1)}, bf16[2,512,512]{2,1,0:T(8,128)(2,1)}, u32[]{:S(2)}) copy-start(bf16[2,512,512]{2,1,0:T(8,128)(2,1)} %param.10) | copy-start | bytes 3145732
  236.6 1.3 copy-start.7
  239.2 697.0 %all-reduce.9.cloned.1.call-start = ((), (), s32[]{:S(2)}) async-start(), calls=%async_computation.2 | async-start | bytes 4194304 | tf_op jit(solution)/shard_map/psum | solution.py:11
  243.6 1.0 copy-start.2
Sparse Core Ops, SparseCore 0:
  10.4 67.5 all-reduce.6
  82.5 151.0 all-reduce.4
  239.3 64.9 all-reduce.10
  308.1 151.9 all-reduce.8
where the time goes:
time: 949 us; the launch traced here: 948 us
  blocking collectives  736 us (78%)
  waiting for transfers between devices  154 us (16%)
  matrix products  28.7 us (3%)
  local copies, waits for them, and re-layouts  13.9 us (1%)
  between operations  13.9 us (1%)
    psum x8, blocking collectives, carry_forward(): row_total = lax.psum(pending, 'pcol')  453 us
    psum x8, blocking collectives, broadcast(): return lax.psum(kept, axis)  217 us
    psum x4, waiting for transfers between devices, broadcast(): return lax.psum(kept, axis)  154 us
    psum x1, blocking collectives, shards(): totals = lax.psum(partial_value, 'pcol')  65.6 us
  transfers between devices with their start and end apart: 4, of which 1 were waited for; matrix products, arithmetic and copies ran while one was open for 3% of the time, Pallas kernels for 0%

commit v1 on v0

--- a/solution.py
+++ b/solution.py
@@ -57,7 +57,7 @@
         pending = lax.dynamic_slice_in_dim(accum, slot_id * blk_width, blk_width, 0)
         res_block = lax.dynamic_slice_in_dim(res_blocks, slot_id, 1, 0)[0]
         inv_block = inverses[0].astype(jnp.float32)
-        row_total = lax.psum(pending, "pcol")
+        row_total = jnp.sum(lax.all_gather(pending, "pcol"), axis=0)
         local_value = jnp.dot(inv_block, res_block - row_total, precision=lax.Precision.HIGHEST)
         new_value = broadcast(local_value, "prow", owner_row)
         rounded = new_value.astype(jnp.bfloat16)

time: 949 us -> 759 us (0.80)
  blocking collectives: 736 us -> 546 us
    psum x8 -> x0, blocking collectives: 453 us -> none  [carry_forward(): row_total = lax.psum(pending, 'pcol')]
    all_gather x0 -> x8, blocking collectives: none -> 285 us  [carry_forward(): row_total = jnp.sum(lax.all_gather(pending, 'pcol'), axis=0)]
    psum x8, blocking collectives: 217 us -> 196 us  [broadcast(): return lax.psum(kept, axis)]
  transfers between devices with their start and end apart: 4 -> 4, of which waited for: 1 -> 1; matrix products, arithmetic and copies ran while one was open for 3% -> 4% of each run, Pallas kernels for 0% -> 0%
where the time goes in v1:
time: 759 us; the launch traced here: 758 us
  blocking collectives  546 us (72%)
  waiting for transfers between devices  154 us (20%)
  matrix products  28.8 us (4%)
  local copies, waits for them, and re-layouts  13.9 us (2%)
  between operations  13.9 us (2%)
    all_gather x8, blocking collectives, carry_forward(): row_total = jnp.sum(lax.all_gather(pending, 'pcol'), axis=0)  285 us
    psum x8, blocking collectives, broadcast(): return lax.psum(kept, axis)  196 us
    psum x4, waiting for transfers between devices, broadcast(): return lax.psum(kept, axis)  154 us
    psum x1, blocking collectives, shards(): totals = lax.psum(partial_value, 'pcol')  65.6 us
  transfers between devices with their start and end apart: 4, of which 1 were waited for; matrix products, arithmetic and copies ran while one was open for 4% of the time, Pallas kernels for 0%

profile of v1, /device:TPU:1, one launch (start us, length us, event | category | flops | bytes accessed | tf_op | source)
XLA Modules:
  0.0 758.2 jit_solution(17645179751813984099)
XLA Ops:
  7.3 2.6 fusion.9
  10.0 2.9 fusion.7
  13.6 65.6 %psum.54 = f32[2048]{0:T(1024)S(1)} all-reduce(f32[2048]{0:T(1024)S(1)} %bitcast.82), channel_id=1, replica_groups=mesh['prow'=8,'pcol'=32] {'pcol'}, use_global_device_ids=true, to_apply=%region_4.5 | all-reduce | flops 2048 | bytes 16384 | tf_op jit(solution)/shard_map/psum | solution.py:45
  79.3 154.3 %all-reduce.5.cloned.1.call-done = bf16[2048,512]{0,1:T(8,128)(2,1)} async-done(((bf16[2048,512]{0,1:T(8,128)(2,1)}), bf16[2048,512]{0,1:T(8,128)(2,1)}) %all-reduce.5.cloned.1.call-update) | async-done | bytes 2097168 | tf_op jit(solution)/shard_map/psum | solution.py:11
  233.6 3.0 subtract_convert_fusion.1
  239.2 4.3 fusion.8
  244.6 502.1 %while.19 = (s32[]{:T(128)}, f32[2048]{0:T(1024)S(1)}, f32[8,512]{1,0:T(8,128)}, s32[]{:T(128)}, f32[4,512]{1,0:T(4,128)S(1)}, /*index=5*/bf16[1,1,512,512]{3,2,...) while((s32[]{:T(128)}, f32[2048]{0:T(1024)S(1)}, ...), condition=%wide.region_8.9_spmd.clone, body=%wide.region_5.8_spmd.clone.sunk | while | flops 5269025 | bytes 2834953 | solution.py:75
  244.7 36.6 %all-gather.4 = f32[32,1,512]{2,1,0:T(1,128)S(1)} all-gather(f32[1,1,512]{2,1,0:T(1,128)S(1)} %bitcast.81), channel_id=2, replica_groups=mesh['prow'=8,'pcol'=32] {'pcol'}, dimensions={0}, use_global_device_ids=true | all-gather | bytes 67584 | tf_op jit(solution)/shard_map/while/body/eval_jaxpr/all_gather | solution.py:60
  281.8 27.2 %psum.57 = f32[512]{0:T(512)S(1)} all-reduce(f32[512]{0:T(512)S(1)} %broadcast_select_fusion.5), channel_id=1, replica_groups=mesh['prow'=8,'pcol'=32] {'prow'}, use_global_device_ids=true, to_apply=%region_7.7 | all-reduce | flops 512 | bytes 4096 | tf_op jit(solution)/shard_map/while/body/eval_jaxpr/psum | solution.py:11
  311.1 37.1 %all-gather.4 = f32[32,1,512]{2,1,0:T(1,128)S(1)} all-gather(f32[1,1,512]{2,1,0:T(1,128)S(1)} %bitcast.81), channel_id=2, replica_groups=mesh['prow'=8,'pcol'=32] {'pcol'}, dimensions={0}, use_global_device_ids=true | all-gather | bytes 67584 | tf_op jit(solution)/shard_map/while/body/eval_jaxpr/all_gather | solution.py:60
  348.9 22.6 %psum.57 = f32[512]{0:T(512)S(1)} all-reduce(f32[512]{0:T(512)S(1)} %broadcast_select_fusion.5), channel_id=1, replica_groups=mesh['prow'=8,'pcol'=32] {'prow'}, use_global_device_ids=true, to_apply=%region_7.7 | all-reduce | flops 512 | bytes 4096 | tf_op jit(solution)/shard_map/while/body/eval_jaxpr/psum | solution.py:11
  373.6 35.5 %all-gather.4 = f32[32,1,512]{2,1,0:T(1,128)S(1)} all-gather(f32[1,1,512]{2,1,0:T(1,128)S(1)} %bitcast.81), channel_id=2, replica_groups=mesh['prow'=8,'pcol'=32] {'pcol'}, dimensions={0}, use_global_device_ids=true | all-gather | bytes 67584 | tf_op jit(solution)/shard_map/while/body/eval_jaxpr/all_gather | solution.py:60
  409.7 24.6 %psum.57 = f32[512]{0:T(512)S(1)} all-reduce(f32[512]{0:T(512)S(1)} %broadcast_select_fusion.5), channel_id=1, replica_groups=mesh['prow'=8,'pcol'=32] {'prow'}, use_global_device_ids=true, to_apply=%region_7.7 | all-reduce | flops 512 | bytes 4096 | tf_op jit(solution)/shard_map/while/body/eval_jaxpr/psum | solution.py:11
  436.3 36.5 %all-gather.4 = f32[32,1,512]{2,1,0:T(1,128)S(1)} all-gather(f32[1,1,512]{2,1,0:T(1,128)S(1)} %bitcast.81), channel_id=2, replica_groups=mesh['prow'=8,'pcol'=32] {'pcol'}, dimensions={0}, use_global_device_ids=true | all-gather | bytes 67584 | tf_op jit(solution)/shard_map/while/body/eval_jaxpr/all_gather | solution.py:60
  473.4 22.5 %psum.57 = f32[512]{0:T(512)S(1)} all-reduce(f32[512]{0:T(512)S(1)} %broadcast_select_fusion.5), channel_id=1, replica_groups=mesh['prow'=8,'pcol'=32] {'prow'}, use_global_device_ids=true, to_apply=%region_7.7 | all-reduce | flops 512 | bytes 4096 | tf_op jit(solution)/shard_map/while/body/eval_jaxpr/psum | solution.py:11
  498.0 35.2 %all-gather.4 = f32[32,1,512]{2,1,0:T(1,128)S(1)} all-gather(f32[1,1,512]{2,1,0:T(1,128)S(1)} %bitcast.81), channel_id=2, replica_groups=mesh['prow'=8,'pcol'=32] {'pcol'}, dimensions={0}, use_global_device_ids=true | all-gather | bytes 67584 | tf_op jit(solution)/shard_map/while/body/eval_jaxpr/all_gather | solution.py:60
  533.8 24.8 %psum.57 = f32[512]{0:T(512)S(1)} all-reduce(f32[512]{0:T(512)S(1)} %broadcast_select_fusion.5), channel_id=1, replica_groups=mesh['prow'=8,'pcol'=32] {'prow'}, use_global_device_ids=true, to_apply=%region_7.7 | all-reduce | flops 512 | bytes 4096 | tf_op jit(solution)/shard_map/while/body/eval_jaxpr/psum | solution.py:11
  560.7 34.3 %all-gather.4 = f32[32,1,512]{2,1,0:T(1,128)S(1)} all-gather(f32[1,1,512]{2,1,0:T(1,128)S(1)} %bitcast.81), channel_id=2, replica_groups=mesh['prow'=8,'pcol'=32] {'pcol'}, dimensions={0}, use_global_device_ids=true | all-gather | bytes 67584 | tf_op jit(solution)/shard_map/while/body/eval_jaxpr/all_gather | solution.py:60
  595.6 24.7 %psum.57 = f32[512]{0:T(512)S(1)} all-reduce(f32[512]{0:T(512)S(1)} %broadcast_select_fusion.5), channel_id=1, replica_groups=mesh['prow'=8,'pcol'=32] {'prow'}, use_global_device_ids=true, to_apply=%region_7.7 | all-reduce | flops 512 | bytes 4096 | tf_op jit(solution)/shard_map/while/body/eval_jaxpr/psum | solution.py:11
  622.4 35.2 %all-gather.4 = f32[32,1,512]{2,1,0:T(1,128)S(1)} all-gather(f32[1,1,512]{2,1,0:T(1,128)S(1)} %bitcast.81), channel_id=2, replica_groups=mesh['prow'=8,'pcol'=32] {'pcol'}, dimensions={0}, use_global_device_ids=true | all-gather | bytes 67584 | tf_op jit(solution)/shard_map/while/body/eval_jaxpr/all_gather | solution.py:60
  658.2 24.8 %psum.57 = f32[512]{0:T(512)S(1)} all-reduce(f32[512]{0:T(512)S(1)} %broadcast_select_fusion.5), channel_id=1, replica_groups=mesh['prow'=8,'pcol'=32] {'prow'}, use_global_device_ids=true, to_apply=%region_7.7 | all-reduce | flops 512 | bytes 4096 | tf_op jit(solution)/shard_map/while/body/eval_jaxpr/psum | solution.py:11
  685.1 34.3 %all-gather.4 = f32[32,1,512]{2,1,0:T(1,128)S(1)} all-gather(f32[1,1,512]{2,1,0:T(1,128)S(1)} %bitcast.81), channel_id=2, replica_groups=mesh['prow'=8,'pcol'=32] {'pcol'}, dimensions={0}, use_global_device_ids=true | all-gather | bytes 67584 | tf_op jit(solution)/shard_map/while/body/eval_jaxpr/all_gather | solution.py:60
  720.0 24.7 %psum.57 = f32[512]{0:T(512)S(1)} all-reduce(f32[512]{0:T(512)S(1)} %broadcast_select_fusion.5), channel_id=1, replica_groups=mesh['prow'=8,'pcol'=32] {'prow'}, use_global_device_ids=true, to_apply=%region_7.7 | all-reduce | flops 512 | bytes 4096 | tf_op jit(solution)/shard_map/while/body/eval_jaxpr/psum | solution.py:11
  746.7 5.0 subtract_convert_fusion
  (114 shorter events, 25.9 us)
Async XLA Ops:
  7.2 5.8 copy-start
  7.2 2.8 copy-start.1
  7.2 2.8 copy-start.6
  7.2 72.0 %all-reduce.7.cloned.1.call-start = ((), (), s32[]{:S(2)}) async-start(), calls=%async_computation.1 | async-start | bytes 1048576 | tf_op jit(solution)/shard_map/psum | solution.py:11
  9.9 223.7 %all-reduce.5.cloned.1.call-start = ((), (), s32[]{:S(2)}) async-start(), calls=%async_computation | async-start | bytes 4194304 | tf_op jit(solution)/shard_map/psum | solution.py:11
  12.8 66.3 %copy-start.4 = (f32[4,1,512]{2,1,0:T(1,128)S(1)}, f32[4,1,512]{2,1,0:T(1,128)}, u32[]{:S(2)}) copy-start(f32[4,1,512]{2,1,0:T(1,128)} %param.12) | copy-start | bytes 24580
  12.9 733.8 %all-reduce.11.cloned.1.call-start = ((), (), s32[]{:S(2)}) async-start(), calls=%async_computation.3 | async-start | bytes 1048576 | tf_op jit(solution)/shard_map/psum | solution.py:11
  79.2 157.4 %copy-start.3 = (f32[2048]{0:T(1024)}, f32[2048]{0:T(1024)S(1)}, u32[]{:S(2)}) copy-start(f32[2048]{0:T(1024)S(1)} %sub.31) | copy-start | bytes 24580
  79.2 158.7 %copy-start.5 = (bf16[2,512,512]{2,1,0:T(8,128)(2,1)S(1)}, bf16[2,512,512]{2,1,0:T(8,128)(2,1)}, u32[]{:S(2)}) copy-start(bf16[2,512,512]{2,1,0:T(8,128)(2,1)} %param.10) | copy-start | bytes 3145732
  236.6 1.3 copy-start.7
  239.2 507.5 %all-reduce.9.cloned.1.call-start = ((), (), s32[]{:S(2)}) async-start(), calls=%async_computation.2 | async-start | bytes 4194304 | tf_op jit(solution)/shard_map/psum | solution.py:11
  243.6 1.0 copy-start.2
Sparse Core Ops, SparseCore 0:
  10.4 67.5 all-reduce.6
  82.5 151.0 all-reduce.4
  239.3 65.1 all-reduce.10
  308.3 151.1 all-reduce.8
